TPU v7x, 32 devices: a whole 2x2x4 slice. The times are simulated.
32 devices in a mesh: group: 2 (over y), leaf: 8 (over z, x), rhs: 2 (over core).
Axes of the slice: x: 2, y: 2, z: 4, core: 2. Of those that a mesh axis runs over, the one named last changes fastest.
Arguments:
- iterate: float32 [128, 16384], P(('group', 'rhs'), 'leaf'), parts along dimension 0, may hold values from -6 to 6
- target: float32 [128, 16384], P(('group', 'rhs'), 'leaf'), parts along dimension 0
- coords: int32 [3, 32768], P(None, ('group', 'leaf')), parts along dimension 1, may hold values from 0 to 63
- tree_order: int32 [16, 2048], P(('group', 'leaf')), parts along dimension 0, may hold values from 0 to 2047, each once within a row
- leaf_basis: bfloat16 [32768, 256], P(('group', 'leaf')), parts along dimension 0, may hold values from -0.125 to 0.125
- transfer: bfloat16 [16, 2, 256, 256], P(('group', 'leaf')), parts along dimension 0, as said below
- coupling: bfloat16 [16, 3, 256, 256], P(('group', 'leaf')), parts along dimension 0, as said below
Outputs:
- direction: float32 [128, 16384], P(('group', 'rhs'), 'leaf'), parts along dimension 0
There are 2 independent parts, one for each index of `group`. A program takes and returns all parts, laid end to end along the dimension named above; each array names one. Nothing has to cross between parts.
Inputs may be any that keep to these rules, and one draw needn't show every extreme that they name: transfer[j, k] is the same for all leaves j that share their level-k node (equal j // 2**k). coupling[j, k] is the same for all leaves j that share their level-k node (equal j // 2**k).
All inputs are finite; a program needn't handle non-finite values.
Results may differ from a plain program's by a relative error of at most 0.0016.
Values sent between devices are 32-bit elements; how exact they have to be, the bound alone decides.
A program may use at most 64 MiB of HBM per device.

v0:
```python
import jax
import jax.numpy as jnp
from jax import lax
from jax.sharding import PartitionSpec as P


def swapped(value, axis, stride):
    mask = 2**stride
    pairs = [(source, source ^ mask) for source in range(lax.axis_size(axis))]
    return lax.ppermute(value, axis, pairs)


def product(left, right):
    return jnp.dot(left, right, precision=lax.Precision.HIGHEST)


def matern_block(left_coords, right_coords):
    squared = (left_coords[0][:, None] - right_coords[0][None, :]) ** 2
    squared = squared + (left_coords[1][:, None] - right_coords[1][None, :]) ** 2
    squared = squared + (left_coords[2][:, None] - right_coords[2][None, :]) ** 2
    scaled = jnp.sqrt(3.0 * squared) * 0.0625
    return (1.0 + scaled) * jnp.exp(-scaled)


def near_field(values, points):
    width = values.shape[1]
    block_rows = min(512, width)

    def accumulate(step_number, running):
        offset = step_number * block_rows
        rows_points = lax.dynamic_slice_in_dim(points, offset, block_rows, 1)
        rows_values = lax.dynamic_slice_in_dim(values, offset, block_rows, 1)
        kernel = matern_block(rows_points, points)
        return running + product(rows_values, kernel)

    summed = lax.fori_loop(0, width // block_rows, accumulate, jnp.zeros(values.shape, jnp.float32))
    return 0.0625 * summed


def pair_step(skeleton, height, tables, couplings, final):
    if final:
        payload = skeleton[None]
    else:
        lifted = product(skeleton, tables[height])
        payload = jnp.stack([skeleton, lifted])
    arrived = swapped(payload, "leaf", height)
    coupled_term = product(arrived[0], couplings[height])
    if final:
        return (coupled_term, skeleton)
    return (coupled_term, lifted + arrived[1])


def local(iterate, target, coords, tree_order, leaf_basis, transfer, coupling):
    devices = lax.axis_size("leaf")
    levels_total = devices.bit_length() - 1
    shuffle = tree_order[0]
    outgoing = (iterate[:, shuffle], coords[:, shuffle].astype(jnp.float32))
    tree_values, tree_coords = (
        lax.all_to_all(outgoing[0], "leaf", split_axis=1, concat_axis=1, tiled=True),
        lax.all_to_all(outgoing[1], "leaf", split_axis=1, concat_axis=1, tiled=True),
    )
    nearby = near_field(tree_values, tree_coords)
    skeleton = jnp.dot(
        tree_values.astype(jnp.bfloat16), leaf_basis, preferred_element_type=jnp.float32
    )
    tables = transfer[0].astype(jnp.float32)
    couplings = coupling[0].astype(jnp.float32)
    coupled = []
    for height in range(levels_total):
        coupled_term, skeleton = pair_step(
            skeleton, height, tables, couplings, height == levels_total - 1
        )
        coupled.append(coupled_term)
    downward = coupled[-1]
    for height in range(levels_total - 2, -1, -1):
        lowered = lax.dot_general(
            downward, tables[height], (((1,), (1,)), ((), ())), precision=lax.Precision.HIGHEST
        )
        downward = coupled[height] + lowered
    far_field = lax.dot_general(
        downward.astype(jnp.bfloat16),
        leaf_basis,
        (((1,), (1,)), ((), ())),
        preferred_element_type=jnp.float32,
    )
    applied = nearby + far_field
    returned = lax.all_to_all(applied, "leaf", split_axis=1, concat_axis=1, tiled=True)
    placed = jnp.zeros_like(target).at[:, shuffle].set(returned)
    residual = target - placed
    power = lax.psum(jnp.sum(residual * residual, axis=1), "leaf")
    return residual / jnp.sqrt(power / (target.shape[1] * devices) + 1e-06)[:, None]


def solution(mesh):
    placed = (
        P(("group", "rhs"), "leaf"),
        P(("group", "rhs"), "leaf"),
        P(None, ("group", "leaf")),
        P(("group", "leaf"), None),
        P(("group", "leaf"), None),
        P(("group", "leaf"), None, None, None),
        P(("group", "leaf"), None, None, None),
    )
    return jax.shard_map(
        local, mesh=mesh, in_specs=placed, out_specs=P(("group", "rhs"), "leaf"), check_vma=False
    )
```

profile of v0, /device:TPU:0, one launch (start us, length us, event | category | flops | bytes accessed | tf_op | source)
XLA Modules:
  0.0 115.0 jit_solution(4000668336593586181)
XLA Ops:
  0.0 0.0 copy-start
  0.0 0.8 compare_select_fusion
  0.8 1.3 %copy.39 = f32[32,2048]{0,1:T(8,128)S(1)} copy(f32[32,2048]{1,0:T(8,128)} %param.9) | data formatting | bytes 524288 | tf_op args[0]
  2.1 5.5 %gather_fusion = f32[2048,32]{1,0:T(8,128)S(1)} fusion(f32[32,2048]{0,1:T(8,128)S(1)} %copy.39, s32[2048]{0:T(1024)S(1)} %broadcast_clamp_fusion), kind=kCustom, calls=%fused_computation | custom fusion | bytes 532480 | tf_op jit(solution)/shard_map/gather | solution.py:57
  7.6 0.3 copy.40
  7.9 16.0 %all_to_all.33 = f32[32,8,256]{2,0,1:T(8,128)S(1)} all-to-all(f32[32,8,256]{2,0,1:T(8,128)S(1)} %copy.40), channel_id=1, replica_groups=mesh['group'=2,'leaf'=8,'rhs'=2] {'leaf'}, dimensions={1} | all-to-all | bytes 524288 | tf_op jit(solution)/shard_map/all_to_all | solution.py:59
  23.8 0.0 copy-start.1
  23.9 0.0 copy-start.2
  23.9 0.0 copy-done
  23.9 0.0 copy-start.5
  23.9 0.3 fusion.51
  24.2 0.7 copy-done.1
  24.9 0.2 fusion.46
  25.1 1.5 %collective-permute-start = (f32[2,32,256]{2,1,0:T(8,128)S(1)}, f32[2,32,256]{2,1,0:T(8,128)S(1)}, u32[]{:S(2)}, u32[]{:S(2)}) collective-permute-start(f32[2,32,256]{2,1,0:T(8,128)S(1)} %pad_maximum_fusion), channel_id=1, source_target_pairs={{0,2},{2,0},{4,6},{6,4},{8,10},{10,8},{12,14},{14,12},{1,3},{3,1},... | collective-permute-start | bytes 196616 | tf_op jit(solution)/shard_map/ppermute | solution.py:10
  26.6 2.9 %collective-permute-done = f32[2,32,256]{2,1,0:T(8,128)S(1)} collective-permute-done((f32[2,32,256]{2,1,0:T(8,128)S(1)}, f32[2,32,256]{2,1,0:T(8,128)S(1)}, u32[]{:S(2)}, u32[]{:S(2)}) %collective-permute-start) | collective-permute-done | bytes 65568 | tf_op jit(solution)/shard_map/ppermute | solution.py:10
  29.4 0.2 fusion.41
  29.7 0.6 pad_maximum_fusion.1
  30.3 0.0 copy-done.2
  30.3 1.1 collective-permute-start.1
  31.3 0.0 copy-done.5
  31.3 0.4 copy.42
  31.7 5.5 %gather_fusion.1 = s32[2048,3]{1,0:T(8,128)S(1)} fusion(s32[3,2048]{0,1:T(8,128)S(1)} %copy.42, s32[2048]{0:T(1024)S(1)} %broadcast_clamp_fusion), kind=kCustom, calls=%fused_computation.1 | custom fusion | bytes 57344 | tf_op jit(solution)/shard_map/gather | solution.py:57
  37.2 0.1 convert_element_type.19
  37.3 0.9 copy.43
  38.2 3.3 %all-to-all-start.1 = ((f32[3,8,256]{2,0,1:T(4,128)}), f32[3,8,256]{2,0,1:T(4,128)S(1)}, u32[]{:S(2)}, u32[]{:S(2)}) async-start(f32[3,8,256]{2,0,1:T(4,128)} %copy.43), calls=%async_computation.1 | async-start | bytes 65536 | tf_op jit(solution)/shard_map/all_to_all | solution.py:60
  41.5 0.0 collective-permute-done.1
  41.6 0.8 fusion.58
  42.3 2.8 %collective-permute-start.2 = (f32[1,32,256]{2,1,0:T(8,128)S(1)}, f32[1,32,256]{2,1,0:T(8,128)S(1)}, u32[]{:S(2)}, u32[]{:S(2)}) collective-permute-start(f32[1,32,256]{2,1,0:T(8,128)S(1)} %fusion.58), channel_id=1, source_target_pairs={{0,8},{2,10},{4,12},{6,14},{8,0},{10,2},{12,4},{14,6},{1,9},{3,11}... | collective-permute-start | bytes 98312 | tf_op jit(solution)/shard_map/ppermute | solution.py:10
  45.1 3.0 %all-to-all-done.1 = f32[3,8,256]{2,0,1:T(4,128)S(1)} async-done(((f32[3,8,256]{2,0,1:T(4,128)}), f32[3,8,256]{2,0,1:T(4,128)S(1)}, u32[]{:S(2)}, u32[]{:S(2)}) %all-to-all-start.1) | async-done | bytes 24608 | tf_op jit(solution)/shard_map/all_to_all | solution.py:60
  48.2 0.0 copy-start.3
  48.2 27.6 %while.14 = (s32[]{:T(128)}, f32[32,2048]{1,0:T(8,128)S(1)}, f32[32,2048]{1,0:T(8,128)}, f32[3,2048]{1,0:T(4,128)S(1)}, s32[]{:T(128)}, /*index=5*/s32[]{:T(128)}, s32[]{:T(128)}, s32[]{:T(128)}, s32[]{}, s32[]{}) while((s32[]{:T(128)}, f32[32,2048]{1,0:T(8,128)S(1)}, f32[32,2048]{1,0:T(8,128)}, f32[3,2048]{1,0:T(4,128)S(1)}, ...), condition=%wide.region_1.0_spmd.clone, body=%wide.region_0.0_spmd.clone.sunk | while | flops 416415744 | bytes 682181 | solution.py:36
  48.2 0.1 constant_dynamic-slice_fusion.2
  48.3 6.8 %fusion.77 = f32[32,2048]{1,0:T(8,128)S(1)} fusion(f32[2048]{0:T(1024)S(1)} %bitcast.106, f32[512]{0:T(512)S(1)} %bitcast.110, f32[2048]{0:T(1024)S(1)} %bitcast.107, f32[512]{0:T(512)S(1)} %bitcast.109, f32[2048]{0:T(1024)S(1)} %bitcast.105, f32[512]{0:T(512)S(1)} %bitcast.108, f32[32,2048]{1,0:T(8,128)S(1)} %get-tuple-element.164, ...), kind=kOutput, calls=%fused_computation.19.clone.1 | convolution fusion | flops 416415744 | bytes 620549 | tf_op jit(solution)/shard_map/while/body/eval_jaxpr/dot_general | solution.py:14
  55.1 0.1 constant_dynamic-slice_fusion.2
  55.2 6.8 %fusion.77 = f32[32,2048]{1,0:T(8,128)S(1)} fusion(f32[2048]{0:T(1024)S(1)} %bitcast.106, f32[512]{0:T(512)S(1)} %bitcast.110, f32[2048]{0:T(1024)S(1)} %bitcast.107, f32[512]{0:T(512)S(1)} %bitcast.109, f32[2048]{0:T(1024)S(1)} %bitcast.105, f32[512]{0:T(512)S(1)} %bitcast.108, f32[32,2048]{1,0:T(8,128)S(1)} %get-tuple-element.164, ...), kind=kOutput, calls=%fused_computation.19.clone.1 | convolution fusion | flops 416415744 | bytes 620549 | tf_op jit(solution)/shard_map/while/body/eval_jaxpr/dot_general | solution.py:14
  62.0 0.1 constant_dynamic-slice_fusion.2
  62.1 6.8 %fusion.77 = f32[32,2048]{1,0:T(8,128)S(1)} fusion(f32[2048]{0:T(1024)S(1)} %bitcast.106, f32[512]{0:T(512)S(1)} %bitcast.110, f32[2048]{0:T(1024)S(1)} %bitcast.107, f32[512]{0:T(512)S(1)} %bitcast.109, f32[2048]{0:T(1024)S(1)} %bitcast.105, f32[512]{0:T(512)S(1)} %bitcast.108, f32[32,2048]{1,0:T(8,128)S(1)} %get-tuple-element.164, ...), kind=kOutput, calls=%fused_computation.19.clone.1 | convolution fusion | flops 416415744 | bytes 620549 | tf_op jit(solution)/shard_map/while/body/eval_jaxpr/dot_general | solution.py:14
  68.9 0.1 constant_dynamic-slice_fusion.2
  69.0 6.8 %fusion.77 = f32[32,2048]{1,0:T(8,128)S(1)} fusion(f32[2048]{0:T(1024)S(1)} %bitcast.106, f32[512]{0:T(512)S(1)} %bitcast.110, f32[2048]{0:T(1024)S(1)} %bitcast.107, f32[512]{0:T(512)S(1)} %bitcast.109, f32[2048]{0:T(1024)S(1)} %bitcast.105, f32[512]{0:T(512)S(1)} %bitcast.108, f32[32,2048]{1,0:T(8,128)S(1)} %get-tuple-element.164, ...), kind=kOutput, calls=%fused_computation.19.clone.1 | convolution fusion | flops 416415744 | bytes 620549 | tf_op jit(solution)/shard_map/while/body/eval_jaxpr/dot_general | solution.py:14
  75.8 0.0 collective-permute-done.2
  75.8 0.0 copy-done.3
  75.8 0.2 fusion.36
  76.0 0.3 fusion.39
  76.3 1.0 convolution_add_fusion.1
  77.2 0.3 fusion.44
  77.5 0.2 fusion.33
  77.7 0.4 convolution_add_fusion
  78.1 10.6 %all_to_all.34 = f32[32,8,256]{2,0,1:T(8,128)S(1)} all-to-all(f32[32,8,256]{2,0,1:T(8,128)S(1)} %bitcast.98), channel_id=1, replica_groups=mesh['group'=2,'leaf'=8,'rhs'=2] {'leaf'}, dimensions={1} | all-to-all | bytes 524288 | tf_op jit(solution)/shard_map/all_to_all | solution.py:87
  88.8 0.3 copy.46
  89.1 0.0 copy-start.4
  89.1 5.8 %scatter_custom_fusion = f32[32,2048]{0,1:T(8,128)S(1)} fusion(s32[2048]{0:T(1024)S(1)} %bitcast.112, f32[2048,32]{1,0:T(8,128)S(1)} %copy.46, f32[]{:T(128)} %constant.55.clone.1), kind=kCustom, calls=%fused_computation.39 | custom fusion | bytes 262148 | tf_op jit(solution)/shard_map/scatter | solution.py:88
  95.0 0.3 copy.47
  95.3 0.0 copy-done.4
  95.3 0.1 multiply_reduce_fusion
  95.5 18.7 %psum.7 = f32[32]{0:T(128)S(1)} all-reduce(f32[32]{0:T(128)S(1)} %get-tuple-element.108), channel_id=1, replica_groups=mesh['group'=2,'leaf'=8,'rhs'=2] {'leaf'}, use_global_device_ids=true, to_apply=%region_4.0 | all-reduce | flops 32 | bytes 256 | tf_op jit(solution)/shard_map/psum | solution.py:90
  114.2 0.8 broadcast_divide_fusion
  (12 shorter events, 0.2 us)
Async XLA Ops:
  0.0 23.9 %copy-start = (bf16[2048,256]{1,0:T(8,128)(2,1)S(1)}, bf16[2048,256]{1,0:T(8,128)(2,1)}, u32[]{:S(2)}) copy-start(bf16[2048,256]{1,0:T(8,128)(2,1)} %param.13) | copy-start | bytes 3145732
  23.8 1.0 copy-start.1
  23.9 6.4 %copy-start.2 = (f32[8,4,8,256]{3,2,0,1:T(8,128)}, f32[8,4,8,256]{3,2,0,1:T(8,128)S(1)}, u32[]{:S(2)}) copy-start(f32[8,4,8,256]{3,2,0,1:T(8,128)S(1)} %copy.49) | copy-start | bytes 786436
  23.9 7.5 %copy-start.5 = (s32[3,2048]{1,0:T(4,128)S(1)}, s32[3,2048]{1,0:T(4,128)}, u32[]{:S(2)}) copy-start(s32[3,2048]{1,0:T(4,128)} %param.11) | copy-start | bytes 73732
  25.1 4.3 %collective-permute-start = (f32[2,32,256]{2,1,0:T(8,128)S(1)}, f32[2,32,256]{2,1,0:T(8,128)S(1)}, u32[]{:S(2)}, u32[]{:S(2)}) collective-permute-start(f32[2,32,256]{2,1,0:T(8,128)S(1)} %pad_maximum_fusion), channel_id=1, source_target_pairs={{0,2},{2,0},{4,6},{6,4},{8,10},{10,8},{12,14},{14,12},{1,3},{3,1},... | collective-permute-start | bytes 196616 | tf_op jit(solution)/shard_map/ppermute | solution.py:10
  30.3 11.3 %collective-permute-start.1 = (f32[2,32,256]{2,1,0:T(8,128)}, f32[2,32,256]{2,1,0:T(8,128)}, u32[]{:S(2)}, u32[]{:S(2)}) collective-permute-start(f32[2,32,256]{2,1,0:T(8,128)} %pad_maximum_fusion.1), channel_id=1, source_target_pairs={{0,4},{2,6},{4,0},{6,2},{8,12},{10,14},{12,8},{14,10},{1,5},{3,7},... | collective-permute-start | bytes 196616 | tf_op jit(solution)/shard_map/ppermute | solution.py:10
  38.2 10.0 %all-to-all-start.1 = ((f32[3,8,256]{2,0,1:T(4,128)}), f32[3,8,256]{2,0,1:T(4,128)S(1)}, u32[]{:S(2)}, u32[]{:S(2)}) async-start(f32[3,8,256]{2,0,1:T(4,128)} %copy.43), calls=%async_computation.1 | async-start | bytes 65536 | tf_op jit(solution)/shard_map/all_to_all | solution.py:60
  42.3 33.4 %collective-permute-start.2 = (f32[1,32,256]{2,1,0:T(8,128)S(1)}, f32[1,32,256]{2,1,0:T(8,128)S(1)}, u32[]{:S(2)}, u32[]{:S(2)}) collective-permute-start(f32[1,32,256]{2,1,0:T(8,128)S(1)} %fusion.58), channel_id=1, source_target_pairs={{0,8},{2,10},{4,12},{6,14},{8,0},{10,2},{12,4},{14,6},{1,9},{3,11}... | collective-permute-start | bytes 98312 | tf_op jit(solution)/shard_map/ppermute | solution.py:10
  48.2 27.6 %copy-start.3 = (bf16[1,3,256,256]{3,2,1,0:T(8,128)(2,1)S(1)}, bf16[1,3,256,256]{3,2,1,0:T(8,128)(2,1)}, u32[]{:S(2)}) copy-start(bf16[1,3,256,256]{3,2,1,0:T(8,128)(2,1)} %param.15) | copy-start | bytes 1179652
  89.1 6.2 %copy-start.4 = (f32[32,2048]{1,0:T(8,128)S(1)}, f32[32,2048]{1,0:T(8,128)}, u32[]{:S(2)}) copy-start(f32[32,2048]{1,0:T(8,128)} %param.10) | copy-start | bytes 786436
where the time goes:
time: 116 us; the launch traced here: 115 us
  blocking collectives  45.3 us (39%)
  matrix products  30 us (26%)
  local copies, waits for them, and re-layouts  21.5 us (19%)
  starting transfers between devices  8.69 us (7%)
  waiting for transfers between devices  5.87 us (5%)
  other arithmetic  3.24 us (3%)
    dot_general x9, matrix products, product(): return jnp.dot(left, right, precision=lax.Precision.HIGHEST)  28.8 us
    psum x1, blocking collectives, local(): power = lax.psum(jnp.sum(residual * residual, axis=1), 'leaf')  18.7 us
    all_to_all x1, blocking collectives, local(): lax.all_to_all(outgoing[0], 'leaf', split_axis=1, concat_axis=1, tiled=True)  16 us
    gather x2, local copies, waits for them, and re-layouts, local(): outgoing = (iterate[:, shuffle], coords[:, shuffle].astype(jnp.float32))  10.9 us
    all_to_all x1, blocking collectives, local(): lax.all_to_all(applied, 'leaf', split_axis=1, concat_axis=1, tiled=True)  10.6 us
    scatter x2, local copies, waits for them, and re-layouts, local(): placed = jnp.zeros_like(target).at[:, shuffle].set(returned)  6.15 us
    ppermute x3, starting transfers between devices, swapped(): return lax.ppermute(value, axis, pairs)  5.36 us
    all_to_all x1, starting transfers between devices, local(): lax.all_to_all(outgoing[1], 'leaf', split_axis=1, concat_axis=1, tiled=True)  3.33 us
  transfers between devices with their start and end apart: 4, of which 2 were waited for; matrix products, arithmetic and copies ran while one was open for 30% of the time, Pallas kernels for 0%

commit v1 on v0

--- a/solution.py
+++ b/solution.py
@@ -1,7 +1,284 @@
+import functools
 import jax
 import jax.numpy as jnp
 from jax import lax
+from jax.experimental import pallas as pl
+from jax.experimental.pallas import tpu as pltpu
 from jax.sharding import PartitionSpec as P
+
+F32 = jnp.float32
+BF16 = jnp.bfloat16
+MESH = pl.DeviceIdType.MESH
+ROWS_T = (((1,), (1,)), ((), ()))
+COLS_T = (((0,), (0,)), ((), ()))
+
+
+def far_first(t, n):
+    if n == 2:
+        return 1 - t
+    return n // 2 + ((t + 1) // 2) * (1 - 2 * (t % 2))
+
+
+def halves(x):
+    high = x.astype(BF16)
+    low = (x - high.astype(F32)).astype(BF16)
+    return jnp.concatenate([high, low], axis=0)
+
+
+def split_dot(x, right, dims):
+    rows = x.shape[0]
+    both = lax.dot_general(halves(x), right, dims, preferred_element_type=F32)
+    return both[:rows] + both[rows:]
+
+
+def fused(
+    n, levels, eval_blocks,
+    iterate, target, coords, order, basis, transfer, coupling,
+    out,
+    parts, coord_rows, onehot, send_values, send_coords, tree_values, tree_coords,
+    left_feat, right_feat, left_t, kernel_k, skel_send, skel_recv, lift_send, lift_recv,
+    applied, returned, placed, power_send, power_recv,
+    c_ss, c_rs, v_ss, v_rs, s_ss, s_rs, l_ss, l_rs, b_ss, b_rs, p_ss, p_rs,
+):
+    rhs, width = iterate.shape
+    share = width // n
+    me = lax.axis_index("leaf")
+
+    def peer(offset):
+        return lax.rem(me + offset, n)
+
+    def source(offset):
+        return lax.rem(me + n - offset, n)
+
+    def cols(index):
+        return pl.ds(pl.multiple_of(index * share, share), share)
+
+    barrier = pltpu.get_barrier_semaphore()
+    for offset in range(1, n):
+        pl.semaphore_signal(barrier, inc=1, device_id={"leaf": peer(offset)}, device_id_type=MESH)
+
+    parts[0:2 * rhs, :] = halves(iterate[...])
+    coord_rows[...] = jnp.zeros_like(coord_rows)
+    coord_rows[0:3, :] = coords[...].astype(F32)
+    parts[2 * rhs:2 * rhs + 16, :] = coord_rows[...].astype(BF16)
+
+    def coord_copy(d):
+        return pltpu.make_async_remote_copy(
+            src_ref=send_coords.at[d], dst_ref=tree_coords.at[:, cols(me)],
+            send_sem=c_ss.at[d], recv_sem=c_rs.at[d],
+            device_id={"leaf": peer(d)}, device_id_type=MESH)
+
+    def value_copy(d):
+        return pltpu.make_async_remote_copy(
+            src_ref=send_values.at[d], dst_ref=tree_values.at[:, cols(me)],
+            send_sem=v_ss.at[d], recv_sem=v_rs.at[d],
+            device_id={"leaf": peer(d)}, device_id_type=MESH)
+
+    for t in range(n):
+        d = far_first(t, n)
+        where = cols(peer(d))
+        spots = lax.broadcasted_iota(jnp.int32, (width, share), 0)
+        chosen = (spots == order[:, where]).astype(F32).astype(BF16)
+        onehot[:, where] = chosen
+        moved = jnp.dot(parts[...], chosen, preferred_element_type=F32)
+        if d:
+            send_values[d] = moved[:rhs] + moved[rhs:2 * rhs]
+            send_coords[d] = moved[2 * rhs:2 * rhs + 8]
+            if t == 0:
+                pl.semaphore_wait(barrier, n - 1)
+            coord_copy(d).start()
+        else:
+            tree_values[:, where] = moved[:rhs] + moved[rhs:2 * rhs]
+            tree_coords[:, where] = moved[2 * rhs:2 * rhs + 8]
+    for t in range(n - 1):
+        value_copy(far_first(t, n)).start()
+
+    for d in range(1, n):
+        coord_copy(d).wait_recv()
+    xyz = tree_coords[0:3, :]
+    norm = jnp.sum(xyz * xyz, axis=0, keepdims=True)
+    norm_high = jnp.floor(norm * (1.0 / 256.0))
+    norm_low = norm - 256.0 * norm_high
+    left_feat[...] = jnp.zeros_like(left_feat)
+    right_feat[...] = jnp.zeros_like(right_feat)
+    left_feat[0:3, :] = xyz
+    left_feat[3:4, :] = norm_low
+    left_feat[4:5, :] = norm_high
+    left_feat[5:6, :] = jnp.full_like(norm, 3.0 / 256.0)
+    left_feat[6:7, :] = jnp.full_like(norm, 3.0)
+    right_feat[0:3, :] = xyz * (-6.0 / 256.0)
+    right_feat[3:4, :] = jnp.full_like(norm, 3.0 / 256.0)
+    right_feat[4:5, :] = jnp.full_like(norm, 3.0)
+    right_feat[5:6, :] = norm_low
+    right_feat[6:7, :] = norm_high
+    left_t[...] = left_feat[...].T.astype(BF16)
+
+    rows_step = 256
+
+    def matern_column(t):
+        where = cols(peer(far_first(t, n)))
+        right = right_feat[:, where].astype(BF16)
+
+        @pl.loop(0, width // rows_step)
+        def _(step):
+            rows = pl.ds(pl.multiple_of(step * rows_step, rows_step), rows_step)
+            q = jnp.dot(left_t[rows, :], right, preferred_element_type=F32)
+            s = q * lax.rsqrt(jnp.maximum(q, 1e-30))
+            kernel_k[rows, where] = ((1.0 + s) * jnp.exp2(s * (-1.4426950408889634))).astype(BF16)
+
+    done = 0
+
+    def matern_until(count):
+        nonlocal done
+        while done < min(count, n):
+            matern_column(done)
+            done += 1
+
+    matern_until(eval_blocks[0])
+
+    for d in range(1, n):
+        value_copy(d).wait_recv()
+    skeleton = jnp.dot(tree_values[...].astype(BF16), basis[...], preferred_element_type=F32)
+
+    def tree_copy(send, recv, ss, rs, height):
+        stride = 2 ** height
+        partner = me + stride * (1 - 2 * lax.rem(me // stride, 2))
+        return pltpu.make_async_remote_copy(
+            src_ref=send.at[height], dst_ref=recv.at[height],
+            send_sem=ss.at[height], recv_sem=rs.at[height],
+            device_id={"leaf": partner}, device_id_type=MESH)
+
+    coupled = []
+    plain = (((1,), (0,)), ((), ()))
+    for height in range(levels):
+        last = height == levels - 1
+        skel_copy = tree_copy(skel_send, skel_recv, s_ss, s_rs, height)
+        skel_send[height] = skeleton
+        skel_copy.start()
+        if not last:
+            lifted = split_dot(skeleton, transfer[0, height], plain)
+            lift_send[height] = lifted
+            lift_copy = tree_copy(lift_send, lift_recv, l_ss, l_rs, height)
+            lift_copy.start()
+        matern_until(eval_blocks[min(height + 1, len(eval_blocks) - 1)])
+        if last:
+            matern_until(n)
+        skel_copy.wait_recv()
+        coupled.append(split_dot(skel_recv[height], coupling[0, height], plain))
+        if not last:
+            lift_copy.wait_recv()
+            skeleton = lifted + lift_recv[height]
+    downward = coupled[-1]
+    for height in range(levels - 2, -1, -1):
+        downward = coupled[height] + split_dot(downward, transfer[0, height], ROWS_T)
+    down = downward.astype(BF16)
+
+    def back_copy(d):
+        return pltpu.make_async_remote_copy(
+            src_ref=applied.at[d], dst_ref=returned.at[:, cols(me)],
+            send_sem=b_ss.at[d], recv_sem=b_rs.at[d],
+            device_id={"leaf": peer(d)}, device_id_type=MESH)
+
+    values = halves(tree_values[...])
+    for t in range(n):
+        d = far_first(t, n)
+        where = cols(peer(d))
+        near = jnp.dot(values, kernel_k[:, where], preferred_element_type=F32)
+        far = lax.dot_general(down, basis[cols(peer(d)), :], ROWS_T, preferred_element_type=F32)
+        total = 0.0625 * (near[:rhs] + near[rhs:]) + far
+        if d:
+            applied[d] = total
+            back_copy(d).start()
+        else:
+            returned[:, where] = total
+
+    def put_back(index):
+        where = cols(index)
+        return lax.dot_general(halves(returned[:, where]), onehot[:, where], ROWS_T,
+                               preferred_element_type=F32)
+
+    placed[...] = put_back(me)
+    for t in range(n - 2, -1, -1):
+        d = far_first(t, n)
+        back_copy(d).wait_recv()
+        placed[...] += put_back(source(d))
+    residual = target[...] - (placed[:rhs] + placed[rhs:])
+    power = jnp.sum(residual * residual, axis=1, keepdims=True)
+
+    tall = jnp.broadcast_to(power, (rhs, 128))
+    square = jnp.concatenate([tall] * (128 // rhs), axis=0)
+    power_send[...] = square.T[0:8, :]
+
+    def power_copy(d):
+        return pltpu.make_async_remote_copy(
+            src_ref=power_send, dst_ref=power_recv.at[d],
+            send_sem=p_ss.at[d], recv_sem=p_rs.at[d],
+            device_id={"leaf": peer(d)}, device_id_type=MESH)
+
+    for t in range(n - 1):
+        power_copy(far_first(t, n)).start()
+    whole = power_send[...]
+    for d in range(1, n):
+        power_copy(d).wait_recv()
+        whole = whole + power_recv[d]
+    total_power = jnp.concatenate([whole] * 16, axis=0).T[0:rhs, 0:1]
+    out[...] = residual * lax.rsqrt(total_power * (1.0 / (width * n)) + 1e-6)
+
+    for d in range(1, n):
+        coord_copy(d).wait_send()
+        value_copy(d).wait_send()
+        back_copy(d).wait_send()
+        power_copy(d).wait_send()
+    for height in range(levels):
+        tree_copy(skel_send, skel_recv, s_ss, s_rs, height).wait_send()
+        if height < levels - 1:
+            tree_copy(lift_send, lift_recv, l_ss, l_rs, height).wait_send()
+
+
+def fused_local(n, iterate, target, coords, tree_order, leaf_basis, transfer, coupling):
+    rhs, width = iterate.shape
+    rank = leaf_basis.shape[1]
+    share = width // n
+    levels = n.bit_length() - 1
+    dma = pltpu.SemaphoreType.DMA
+    vmem = pltpu.VMEM
+    return pl.pallas_call(
+        functools.partial(fused, n, levels, EVAL_BLOCKS),
+        out_shape=jax.ShapeDtypeStruct((rhs, width), F32),
+        in_specs=[pl.BlockSpec(memory_space=vmem)] * 7,
+        out_specs=pl.BlockSpec(memory_space=vmem),
+        scratch_shapes=[
+            vmem((2 * rhs + 16, width), BF16),
+            vmem((16, width), F32),
+            vmem((width, width), BF16),
+            vmem((n, rhs, share), F32),
+            vmem((n, 8, share), F32),
+            vmem((rhs, width), F32),
+            vmem((8, width), F32),
+            vmem((16, width), F32),
+            vmem((16, width), F32),
+            vmem((width, 16), BF16),
+            vmem((width, width), BF16),
+            vmem((levels, rhs, rank), F32),
+            vmem((levels, rhs, rank), F32),
+            vmem((levels, rhs, rank), F32),
+            vmem((levels, rhs, rank), F32),
+            vmem((n, rhs, share), F32),
+            vmem((rhs, width), F32),
+            vmem((2 * rhs, width), F32),
+            vmem((8, 128), F32),
+            vmem((n, 8, 128), F32),
+            dma((n,)), dma((n,)), dma((n,)), dma((n,)),
+            dma((levels,)), dma((levels,)), dma((levels,)), dma((levels,)),
+            dma((n,)), dma((n,)), dma((n,)), dma((n,)),
+        ],
+        compiler_params=pltpu.CompilerParams(
+            collective_id=0, has_side_effects=True, vmem_limit_bytes=50 * 2**20
+        ),
+    )(iterate, target, coords, tree_order, leaf_basis, transfer, coupling)
+
+
+EVAL_BLOCKS = (4, 5, 6, 8)
 
 
 def swapped(value, axis, stride):
@@ -91,6 +368,14 @@
     return residual / jnp.sqrt(power / (target.shape[1] * devices) + 1e-06)[:, None]
 
 
+def by_shape(iterate, *rest):
+    n = lax.axis_size("leaf")
+    rhs, width = iterate.shape
+    if n & (n - 1) == 0 and n > 1 and width % (128 * n) == 0 and rhs % 16 == 0 and 128 % rhs == 0:
+        return fused_local(n, iterate, *rest)
+    return local(iterate, *rest)
+
+
 def solution(mesh):
     placed = (
         P(("group", "rhs"), "leaf"),
@@ -102,5 +387,5 @@
         P(("group", "leaf"), None, None, None),
     )
     return jax.shard_map(
-        local, mesh=mesh, in_specs=placed, out_specs=P(("group", "rhs"), "leaf"), check_vma=False
-    )
+        by_shape, mesh=mesh, in_specs=placed, out_specs=P(("group", "rhs"), "leaf"), check_vma=False
+    )

time: 116 us -> 53.6 us (0.46)
  Pallas kernels: 0 us -> 45.9 us
  blocking collectives: 45.3 us -> 0 us
  matrix products: 30 us -> 0 us
  local copies, waits for them, and re-layouts: 21.5 us -> 7.23 us
  starting transfers between devices: 8.69 us -> 0 us
  waiting for transfers between devices: 5.87 us -> 0 us
  other arithmetic: 3.24 us -> 0 us
    pallas_call x0 -> x1, Pallas kernels: none -> 45.9 us  [fused_local(): pl.pallas_call(functools.partial(fused, n, levels, EVAL_BLOCKS), out_shap...]
    dot_general x13 -> x0, matrix products: 30 us -> none  [the longest x9 28.8 us: product(): return jnp.dot(left, right, precision=lax.Precision.HIGHEST)]
    all_to_all x2 -> x0, blocking collectives: 26.6 us -> none  [the longest x1 16 us: local(): lax.all_to_all(outgoing[0], 'leaf', split_axis=1, concat_axis=1, tiled=True)]
    psum x1 -> x0, blocking collectives: 18.7 us -> none  [local(): power = lax.psum(jnp.sum(residual * residual, axis=1), 'leaf')]
    gather x2 -> x0, local copies, waits for them, and re-layouts: 10.9 us -> none  [local(): outgoing = (iterate[:, shuffle], coords[:, shuffle].astype(jnp.float32))]
    scatter x2 -> x0, local copies, waits for them, and re-layouts: 6.15 us -> none  [local(): placed = jnp.zeros_like(target).at[:, shuffle].set(returned)]
    ppermute x3 -> x0, starting transfers between devices: 5.36 us -> none  [swapped(): return lax.ppermute(value, axis, pairs)]
    unnamed x14 -> x15, local copies, waits for them, and re-layouts: 2.37 us -> 7.23 us
  transfers between devices with their start and end apart: 4 -> 0, of which waited for: 2 -> 0; matrix products, arithmetic and copies ran while one was open for 30% -> 0% of each run, Pallas kernels for 0% -> 0%
where the time goes in v1:
time: 53.6 us; the launch traced here: 53.2 us
  Pallas kernels  45.9 us (86%)
  local copies, waits for them, and re-layouts  7.23 us (13%)
    pallas_call x1, Pallas kernels, fused_local(): pl.pallas_call(functools.partial(fused, n, levels, EVAL_BLOCKS), out_shap...  45.9 us
    unnamed x15, local copies, waits for them, and re-layouts  7.23 us

profile of v1, /device:TPU:0, one launch (start us, length us, event | category | flops | bytes accessed | tf_op | source)
XLA Modules:
  0.0 53.2 jit_solution(3183896536662361975)
XLA Ops:
  0.0 0.0 copy-start
  0.0 1.2 %copy-done = bf16[2048,256]{1,0:T(8,128)(2,1)S(1)} copy-done((bf16[2048,256]{1,0:T(8,128)(2,1)S(1)}, bf16[2048,256]{1,0:T(8,128)(2,1)}, u32[]{:S(2)}) %copy-start) | copy-done | bytes 1048600
  1.2 0.0 copy-start.1
  1.2 1.0 %copy-done.1 = bf16[1,3,256,256]{3,2,1,0:T(8,128)(2,1)S(1)} copy-done((bf16[1,3,256,256]{3,2,1,0:T(8,128)(2,1)S(1)}, bf16[1,3,256,256]{3,2,1,0:T(8,128)(2,1)}, u32[]{:S(2)}) %copy-start.1) | copy-done | bytes 393240
  2.2 0.0 copy-start.2
  2.2 0.9 %copy-done.2 = f32[32,2048]{1,0:T(8,128)S(1)} copy-done((f32[32,2048]{1,0:T(8,128)S(1)}, f32[32,2048]{1,0:T(8,128)}, u32[]{:S(2)}) %copy-start.2) | copy-done | bytes 262168
  3.2 0.0 copy-start.3
  3.2 0.9 %copy-done.3 = f32[32,2048]{1,0:T(8,128)S(1)} copy-done((f32[32,2048]{1,0:T(8,128)S(1)}, f32[32,2048]{1,0:T(8,128)}, u32[]{:S(2)}) %copy-start.3) | copy-done | bytes 262168
  4.1 0.0 copy-start.4
  4.1 0.9 %copy-done.4 = bf16[1,2,256,256]{3,2,1,0:T(8,128)(2,1)S(1)} copy-done((bf16[1,2,256,256]{3,2,1,0:T(8,128)(2,1)S(1)}, bf16[1,2,256,256]{3,2,1,0:T(8,128)(2,1)}, u32[]{:S(2)}) %copy-start.4) | copy-done | bytes 262168
  5.1 0.0 copy-start.5
  5.1 0.8 %copy-done.5 = s32[3,2048]{1,0:T(4,128)S(1)} copy-done((s32[3,2048]{1,0:T(4,128)S(1)}, s32[3,2048]{1,0:T(4,128)}, u32[]{:S(2)}) %copy-start.5) | copy-done | bytes 24600
  5.8 0.0 copy-start.6
  5.8 0.7 %copy-done.6 = s32[1,2048]{1,0:T(1,128)S(1)} copy-done((s32[1,2048]{1,0:T(1,128)S(1)}, s32[1,2048]{1,0:T(1,128)}, u32[]{:S(2)}) %copy-start.6) | copy-done | bytes 8216
  6.5 45.9 %shard_map.73 = f32[32,2048]{1,0:T(8,128)S(1)} custom-call(f32[32,2048]{1,0:T(8,128)S(1)} %copy-done.2, f32[32,2048]{1,0:T(8,128)S(1)} %copy-done.3, s32[3,2048]{1,0:T(4,128)S(1)} %copy-done.5, s32[1,2048]{1,0:T(1,128)S(1)} %copy-done.6, bf16[2048,256]{1,0:T(8,128)(2,1)S(1)} %copy-done, bf16[1,2,256,256]{3,2,1,0:T(8,128)(2,1)S(1)} %copy-done.4, ...), custom_call_target="tpu_custom_call" | custom-call | tf_op jit(solution)/shard_map/pallas_call | solution.py:245
  52.5 0.7 %copy.9 = f32[32,2048]{1,0:T(8,128)} copy(f32[32,2048]{1,0:T(8,128)S(1)} %shard_map.73) | data formatting | bytes 524288
Async XLA Ops:
  0.0 1.2 %copy-start = (bf16[2048,256]{1,0:T(8,128)(2,1)S(1)}, bf16[2048,256]{1,0:T(8,128)(2,1)}, u32[]{:S(2)}) copy-start(bf16[2048,256]{1,0:T(8,128)(2,1)} %basis.1) | copy-start | bytes 3145732
  1.2 1.0 %copy-start.1 = (bf16[1,3,256,256]{3,2,1,0:T(8,128)(2,1)S(1)}, bf16[1,3,256,256]{3,2,1,0:T(8,128)(2,1)}, u32[]{:S(2)}) copy-start(bf16[1,3,256,256]{3,2,1,0:T(8,128)(2,1)} %coupling.1) | copy-start | bytes 1179652
  2.2 0.9 %copy-start.2 = (f32[32,2048]{1,0:T(8,128)S(1)}, f32[32,2048]{1,0:T(8,128)}, u32[]{:S(2)}) copy-start(f32[32,2048]{1,0:T(8,128)} %iterate.1) | copy-start | bytes 786436
  3.2 0.9 %copy-start.3 = (f32[32,2048]{1,0:T(8,128)S(1)}, f32[32,2048]{1,0:T(8,128)}, u32[]{:S(2)}) copy-start(f32[32,2048]{1,0:T(8,128)} %target.1) | copy-start | bytes 786436
  4.1 0.9 %copy-start.4 = (bf16[1,2,256,256]{3,2,1,0:T(8,128)(2,1)S(1)}, bf16[1,2,256,256]{3,2,1,0:T(8,128)(2,1)}, u32[]{:S(2)}) copy-start(bf16[1,2,256,256]{3,2,1,0:T(8,128)(2,1)} %transfer.1) | copy-start | bytes 786436
  5.1 0.8 %copy-start.5 = (s32[3,2048]{1,0:T(4,128)S(1)}, s32[3,2048]{1,0:T(4,128)}, u32[]{:S(2)}) copy-start(s32[3,2048]{1,0:T(4,128)} %coords.1) | copy-start | bytes 73732
  5.8 0.7 %copy-start.6 = (s32[1,2048]{1,0:T(1,128)S(1)}, s32[1,2048]{1,0:T(1,128)}, u32[]{:S(2)}) copy-start(s32[1,2048]{1,0:T(1,128)} %order.1) | copy-start | bytes 24580

commit v2 on v1

--- a/solution.py
+++ b/solution.py
@@ -32,13 +32,14 @@
 
 
 def fused(
-    n, levels, eval_blocks,
+    n, levels,
+    iterate_h, target_h, coords_h, order_h, basis_h, transfer_h, coupling_h,
+    out,
     iterate, target, coords, order, basis, transfer, coupling,
-    out,
     parts, coord_rows, onehot, send_values, send_coords, tree_values, tree_coords,
-    left_feat, right_feat, left_t, kernel_k, skel_send, skel_recv, lift_send, lift_recv,
+    left_feat, right_feat, left_t, kernel_k, skel_send, skel_recv,
     applied, returned, placed, power_send, power_recv,
-    c_ss, c_rs, v_ss, v_rs, s_ss, s_rs, l_ss, l_rs, b_ss, b_rs, p_ss, p_rs,
+    in_s, basis_s, c_ss, c_rs, v_ss, v_rs, s_ss, s_rs, b_ss, b_rs, p_ss, p_rs,
 ):
     rhs, width = iterate.shape
     share = width // n
@@ -53,33 +54,51 @@
     def cols(index):
         return pl.ds(pl.multiple_of(index * share, share), share)
 
+    def slot(index):
+        return slice(index * share, (index + 1) * share)
+
+    whole = (order, iterate, coords, transfer, coupling, target)
+    loads = [
+        pltpu.make_async_copy(src, dst, in_s.at[index]) for index, (src, dst) in enumerate(zip(
+            (order_h, iterate_h, coords_h, transfer_h, coupling_h, target_h), whole))]
+    for load in loads[:3]:
+        load.start()
+    basis_loads = [
+        pltpu.make_async_copy(basis_h.at[cols(source(d)), :], basis.at[slot(d), :], basis_s.at[d])
+        for d in range(n)]
+
     barrier = pltpu.get_barrier_semaphore()
     for offset in range(1, n):
         pl.semaphore_signal(barrier, inc=1, device_id={"leaf": peer(offset)}, device_id_type=MESH)
+    for load in basis_loads + loads[3:]:
+        load.start()
+    coord_rows[...] = jnp.zeros_like(coord_rows)
+    left_feat[...] = jnp.zeros_like(left_feat)
+    right_feat[...] = jnp.zeros_like(right_feat)
+    for load in loads[:3]:
+        load.wait()
 
     parts[0:2 * rhs, :] = halves(iterate[...])
-    coord_rows[...] = jnp.zeros_like(coord_rows)
     coord_rows[0:3, :] = coords[...].astype(F32)
     parts[2 * rhs:2 * rhs + 16, :] = coord_rows[...].astype(BF16)
 
     def coord_copy(d):
         return pltpu.make_async_remote_copy(
-            src_ref=send_coords.at[d], dst_ref=tree_coords.at[:, cols(me)],
+            src_ref=send_coords.at[d], dst_ref=tree_coords.at[:, slot(d)],
             send_sem=c_ss.at[d], recv_sem=c_rs.at[d],
             device_id={"leaf": peer(d)}, device_id_type=MESH)
 
     def value_copy(d):
         return pltpu.make_async_remote_copy(
-            src_ref=send_values.at[d], dst_ref=tree_values.at[:, cols(me)],
+            src_ref=send_values.at[d], dst_ref=tree_values.at[:, slot(d)],
             send_sem=v_ss.at[d], recv_sem=v_rs.at[d],
             device_id={"leaf": peer(d)}, device_id_type=MESH)
 
     for t in range(n):
         d = far_first(t, n)
-        where = cols(peer(d))
         spots = lax.broadcasted_iota(jnp.int32, (width, share), 0)
-        chosen = (spots == order[:, where]).astype(F32).astype(BF16)
-        onehot[:, where] = chosen
+        chosen = (spots == order[:, cols(peer(d))]).astype(F32).astype(BF16)
+        onehot[:, slot(d)] = chosen
         moved = jnp.dot(parts[...], chosen, preferred_element_type=F32)
         if d:
             send_values[d] = moved[:rhs] + moved[rhs:2 * rhs]
@@ -88,10 +107,11 @@
                 pl.semaphore_wait(barrier, n - 1)
             coord_copy(d).start()
         else:
-            tree_values[:, where] = moved[:rhs] + moved[rhs:2 * rhs]
-            tree_coords[:, where] = moved[2 * rhs:2 * rhs + 8]
-    for t in range(n - 1):
-        value_copy(far_first(t, n)).start()
+            tree_values[:, slot(0)] = moved[:rhs] + moved[rhs:2 * rhs]
+            tree_coords[:, slot(0)] = moved[2 * rhs:2 * rhs + 8]
+        if t == n - 2:
+            for u in range(n - 1):
+                value_copy(far_first(u, n)).start()
 
     for d in range(1, n):
         coord_copy(d).wait_recv()
@@ -99,8 +119,6 @@
     norm = jnp.sum(xyz * xyz, axis=0, keepdims=True)
     norm_high = jnp.floor(norm * (1.0 / 256.0))
     norm_low = norm - 256.0 * norm_high
-    left_feat[...] = jnp.zeros_like(left_feat)
-    right_feat[...] = jnp.zeros_like(right_feat)
     left_feat[0:3, :] = xyz
     left_feat[3:4, :] = norm_low
     left_feat[4:5, :] = norm_high
@@ -113,61 +131,62 @@
     right_feat[6:7, :] = norm_high
     left_t[...] = left_feat[...].T.astype(BF16)
 
-    rows_step = 256
-
-    def matern_column(t):
-        where = cols(peer(far_first(t, n)))
-        right = right_feat[:, where].astype(BF16)
-
-        @pl.loop(0, width // rows_step)
-        def _(step):
-            rows = pl.ds(pl.multiple_of(step * rows_step, rows_step), rows_step)
-            q = jnp.dot(left_t[rows, :], right, preferred_element_type=F32)
+    def matern_column(j):
+        right = right_feat[:, slot(j)].astype(BF16)
+        for i in range(j + 1):
+            q = jnp.dot(left_t[slot(i), :], right, preferred_element_type=F32)
             s = q * lax.rsqrt(jnp.maximum(q, 1e-30))
-            kernel_k[rows, where] = ((1.0 + s) * jnp.exp2(s * (-1.4426950408889634))).astype(BF16)
-
-    done = 0
-
-    def matern_until(count):
-        nonlocal done
-        while done < min(count, n):
-            matern_column(done)
-            done += 1
-
-    matern_until(eval_blocks[0])
-
+            kernel_k[slot(i), slot(j)] = ((1.0 + s) * jnp.exp2(s * (-1.4426950408889634))).astype(BF16)
+
+    early = (5 * n) // 8
+    for j in range(early):
+        matern_column(j)
+
+    for load in basis_loads + loads[3:]:
+        load.wait()
     for d in range(1, n):
         value_copy(d).wait_recv()
-    skeleton = jnp.dot(tree_values[...].astype(BF16), basis[...], preferred_element_type=F32)
-
-    def tree_copy(send, recv, ss, rs, height):
-        stride = 2 ** height
-        partner = me + stride * (1 - 2 * lax.rem(me // stride, 2))
+    plain = (((1,), (0,)), ((), ()))
+    skeleton = [jnp.dot(tree_values[...].astype(BF16), basis[...], preferred_element_type=F32)]
+    for height in range(levels - 1):
+        skeleton.append(split_dot(skeleton[height], transfer[0, height], plain))
+    for height in range(levels):
+        skel_send[height] = skeleton[height]
+
+    def tree_copy(height, turn):
+        size = 2 ** height
+        node = me // size
+        sibling = node + 1 - 2 * lax.rem(node, 2)
+        index = size - 1 + turn
         return pltpu.make_async_remote_copy(
-            src_ref=send.at[height], dst_ref=recv.at[height],
-            send_sem=ss.at[height], recv_sem=rs.at[height],
-            device_id={"leaf": partner}, device_id_type=MESH)
-
+            src_ref=skel_send.at[height], dst_ref=skel_recv.at[index],
+            send_sem=s_ss.at[index], recv_sem=s_rs.at[index],
+            device_id={"leaf": sibling * size + lax.rem(me + turn, size)}, device_id_type=MESH)
+
+    tree_copies = [tree_copy(height, turn) for height in reversed(range(levels)) for turn in range(2 ** height)]
+    for copy in tree_copies:
+        copy.start()
+
+    for j in range(early, n):
+        matern_column(j)
+    values = halves(tree_values[...])
+    for j in range(n):
+        cut = (j + 1) * share
+        near = jnp.dot(values[:, :cut], kernel_k[:cut, slot(j)], preferred_element_type=F32)
+        if j < n - 1:
+            near += lax.dot_general(values[:, cut:], kernel_k[slot(j), cut:], ROWS_T,
+                                    preferred_element_type=F32)
+        applied[j] = 0.0625 * (near[:rhs] + near[rhs:])
+
+    for copy in tree_copies:
+        copy.wait_recv()
     coupled = []
-    plain = (((1,), (0,)), ((), ()))
     for height in range(levels):
-        last = height == levels - 1
-        skel_copy = tree_copy(skel_send, skel_recv, s_ss, s_rs, height)
-        skel_send[height] = skeleton
-        skel_copy.start()
-        if not last:
-            lifted = split_dot(skeleton, transfer[0, height], plain)
-            lift_send[height] = lifted
-            lift_copy = tree_copy(lift_send, lift_recv, l_ss, l_rs, height)
-            lift_copy.start()
-        matern_until(eval_blocks[min(height + 1, len(eval_blocks) - 1)])
-        if last:
-            matern_until(n)
-        skel_copy.wait_recv()
-        coupled.append(split_dot(skel_recv[height], coupling[0, height], plain))
-        if not last:
-            lift_copy.wait_recv()
-            skeleton = lifted + lift_recv[height]
+        first = 2 ** height - 1
+        gathered = skel_recv[first]
+        for turn in range(1, 2 ** height):
+            gathered = gathered + skel_recv[first + turn]
+        coupled.append(split_dot(gathered, coupling[0, height], plain))
     downward = coupled[-1]
     for height in range(levels - 2, -1, -1):
         downward = coupled[height] + split_dot(downward, transfer[0, height], ROWS_T)
@@ -175,33 +194,28 @@
 
     def back_copy(d):
         return pltpu.make_async_remote_copy(
-            src_ref=applied.at[d], dst_ref=returned.at[:, cols(me)],
+            src_ref=applied.at[d], dst_ref=returned.at[:, slot(d)],
             send_sem=b_ss.at[d], recv_sem=b_rs.at[d],
-            device_id={"leaf": peer(d)}, device_id_type=MESH)
-
-    values = halves(tree_values[...])
+            device_id={"leaf": source(d)}, device_id_type=MESH)
+
     for t in range(n):
         d = far_first(t, n)
-        where = cols(peer(d))
-        near = jnp.dot(values, kernel_k[:, where], preferred_element_type=F32)
-        far = lax.dot_general(down, basis[cols(peer(d)), :], ROWS_T, preferred_element_type=F32)
-        total = 0.0625 * (near[:rhs] + near[rhs:]) + far
+        far = lax.dot_general(down, basis[slot(d), :], ROWS_T, preferred_element_type=F32)
         if d:
-            applied[d] = total
+            applied[d] += far
             back_copy(d).start()
         else:
-            returned[:, where] = total
-
-    def put_back(index):
-        where = cols(index)
-        return lax.dot_general(halves(returned[:, where]), onehot[:, where], ROWS_T,
+            returned[:, slot(0)] = applied[0] + far
+
+    def put_back(d):
+        return lax.dot_general(halves(returned[:, slot(d)]), onehot[:, slot(d)], ROWS_T,
                                preferred_element_type=F32)
 
-    placed[...] = put_back(me)
+    placed[...] = put_back(0)
     for t in range(n - 2, -1, -1):
         d = far_first(t, n)
         back_copy(d).wait_recv()
-        placed[...] += put_back(source(d))
+        placed[...] += put_back(d)
     residual = target[...] - (placed[:rhs] + placed[rhs:])
     power = jnp.sum(residual * residual, axis=1, keepdims=True)
 
@@ -217,11 +231,11 @@
 
     for t in range(n - 1):
         power_copy(far_first(t, n)).start()
-    whole = power_send[...]
+    summed = power_send[...]
     for d in range(1, n):
         power_copy(d).wait_recv()
-        whole = whole + power_recv[d]
-    total_power = jnp.concatenate([whole] * 16, axis=0).T[0:rhs, 0:1]
+        summed = summed + power_recv[d]
+    total_power = jnp.concatenate([summed] * 16, axis=0).T[0:rhs, 0:1]
     out[...] = residual * lax.rsqrt(total_power * (1.0 / (width * n)) + 1e-6)
 
     for d in range(1, n):
@@ -229,10 +243,8 @@
         value_copy(d).wait_send()
         back_copy(d).wait_send()
         power_copy(d).wait_send()
-    for height in range(levels):
-        tree_copy(skel_send, skel_recv, s_ss, s_rs, height).wait_send()
-        if height < levels - 1:
-            tree_copy(lift_send, lift_recv, l_ss, l_rs, height).wait_send()
+    for copy in tree_copies:
+        copy.wait_send()
 
 
 def fused_local(n, iterate, target, coords, tree_order, leaf_basis, transfer, coupling):
@@ -243,11 +255,18 @@
     dma = pltpu.SemaphoreType.DMA
     vmem = pltpu.VMEM
     return pl.pallas_call(
-        functools.partial(fused, n, levels, EVAL_BLOCKS),
+        functools.partial(fused, n, levels),
         out_shape=jax.ShapeDtypeStruct((rhs, width), F32),
-        in_specs=[pl.BlockSpec(memory_space=vmem)] * 7,
+        in_specs=[pl.BlockSpec(memory_space=pltpu.HBM)] * 7,
         out_specs=pl.BlockSpec(memory_space=vmem),
         scratch_shapes=[
+            vmem(iterate.shape, F32),
+            vmem(target.shape, F32),
+            vmem(coords.shape, jnp.int32),
+            vmem(tree_order.shape, jnp.int32),
+            vmem(leaf_basis.shape, BF16),
+            vmem(transfer.shape, BF16),
+            vmem(coupling.shape, BF16),
             vmem((2 * rhs + 16, width), BF16),
             vmem((16, width), F32),
             vmem((width, width), BF16),
@@ -260,25 +279,20 @@
             vmem((width, 16), BF16),
             vmem((width, width), BF16),
             vmem((levels, rhs, rank), F32),
-            vmem((levels, rhs, rank), F32),
-            vmem((levels, rhs, rank), F32),
-            vmem((levels, rhs, rank), F32),
+            vmem((n, rhs, rank), F32),
             vmem((n, rhs, share), F32),
             vmem((rhs, width), F32),
             vmem((2 * rhs, width), F32),
             vmem((8, 128), F32),
             vmem((n, 8, 128), F32),
+            dma((6,)), dma((n,)),
             dma((n,)), dma((n,)), dma((n,)), dma((n,)),
-            dma((levels,)), dma((levels,)), dma((levels,)), dma((levels,)),
-            dma((n,)), dma((n,)), dma((n,)), dma((n,)),
+            dma((n,)), dma((n,)), dma((n,)), dma((n,)), dma((n,)), dma((n,)),
         ],
         compiler_params=pltpu.CompilerParams(
             collective_id=0, has_side_effects=True, vmem_limit_bytes=50 * 2**20
         ),
     )(iterate, target, coords, tree_order, leaf_basis, transfer, coupling)
-
-
-EVAL_BLOCKS = (4, 5, 6, 8)
 
 
 def swapped(value, axis, stride):

time: 53.6 us -> 45 us (0.84)
  Pallas kernels: 45.9 us -> 37.4 us
    pallas_call x1, Pallas kernels: 45.9 us -> 37.4 us  [fused_local(): pl.pallas_call(functools.partial(fused, n, levels), out_shape=jax.ShapeDt...]
where the time goes in v2:
time: 45 us; the launch traced here: 44.6 us
  Pallas kernels  37.4 us (83%)
  local copies, waits for them, and re-layouts  7.23 us (16%)
    pallas_call x1, Pallas kernels, fused_local(): pl.pallas_call(functools.partial(fused, n, levels), out_shape=jax.ShapeDt...  37.4 us
    unnamed x15, local copies, waits for them, and re-layouts  7.23 us

profile of v2, /device:TPU:0, one launch (start us, length us, event | category | flops | bytes accessed | tf_op | source)
XLA Modules:
  0.0 44.6 jit_solution(7015025286519688030)
XLA Ops:
  0.0 0.0 copy-start
  0.0 1.2 %copy-done = bf16[2048,256]{1,0:T(8,128)(2,1)S(1)} copy-done((bf16[2048,256]{1,0:T(8,128)(2,1)S(1)}, bf16[2048,256]{1,0:T(8,128)(2,1)}, u32[]{:S(2)}) %copy-start) | copy-done | bytes 1048600
  1.2 0.0 copy-start.1
  1.2 1.0 %copy-done.1 = bf16[1,3,256,256]{3,2,1,0:T(8,128)(2,1)S(1)} copy-done((bf16[1,3,256,256]{3,2,1,0:T(8,128)(2,1)S(1)}, bf16[1,3,256,256]{3,2,1,0:T(8,128)(2,1)}, u32[]{:S(2)}) %copy-start.1) | copy-done | bytes 393240
  2.2 0.0 copy-start.2
  2.2 0.9 %copy-done.2 = f32[32,2048]{1,0:T(8,128)S(1)} copy-done((f32[32,2048]{1,0:T(8,128)S(1)}, f32[32,2048]{1,0:T(8,128)}, u32[]{:S(2)}) %copy-start.2) | copy-done | bytes 262168
  3.2 0.0 copy-start.3
  3.2 0.9 %copy-done.3 = f32[32,2048]{1,0:T(8,128)S(1)} copy-done((f32[32,2048]{1,0:T(8,128)S(1)}, f32[32,2048]{1,0:T(8,128)}, u32[]{:S(2)}) %copy-start.3) | copy-done | bytes 262168
  4.1 0.0 copy-start.4
  4.1 0.9 %copy-done.4 = bf16[1,2,256,256]{3,2,1,0:T(8,128)(2,1)S(1)} copy-done((bf16[1,2,256,256]{3,2,1,0:T(8,128)(2,1)S(1)}, bf16[1,2,256,256]{3,2,1,0:T(8,128)(2,1)}, u32[]{:S(2)}) %copy-start.4) | copy-done | bytes 262168
  5.1 0.0 copy-start.5
  5.1 0.8 %copy-done.5 = s32[3,2048]{1,0:T(4,128)S(1)} copy-done((s32[3,2048]{1,0:T(4,128)S(1)}, s32[3,2048]{1,0:T(4,128)}, u32[]{:S(2)}) %copy-start.5) | copy-done | bytes 24600
  5.8 0.0 copy-start.6
  5.8 0.7 %copy-done.6 = s32[1,2048]{1,0:T(1,128)S(1)} copy-done((s32[1,2048]{1,0:T(1,128)S(1)}, s32[1,2048]{1,0:T(1,128)}, u32[]{:S(2)}) %copy-start.6) | copy-done | bytes 8216
  6.5 37.4 %shard_map.73 = f32[32,2048]{1,0:T(8,128)S(1)} custom-call(f32[32,2048]{1,0:T(8,128)S(1)} %copy-done.2, f32[32,2048]{1,0:T(8,128)S(1)} %copy-done.3, s32[3,2048]{1,0:T(4,128)S(1)} %copy-done.5, s32[1,2048]{1,0:T(1,128)S(1)} %copy-done.6, bf16[2048,256]{1,0:T(8,128)(2,1)S(1)} %copy-done, bf16[1,2,256,256]{3,2,1,0:T(8,128)(2,1)S(1)} %copy-done.4, ...), custom_call_target="tpu_custom_call" | custom-call | tf_op jit(solution)/shard_map/pallas_call | solution.py:257
  43.9 0.7 %copy.9 = f32[32,2048]{1,0:T(8,128)} copy(f32[32,2048]{1,0:T(8,128)S(1)} %shard_map.73) | data formatting | bytes 524288
Async XLA Ops:
  0.0 1.2 %copy-start = (bf16[2048,256]{1,0:T(8,128)(2,1)S(1)}, bf16[2048,256]{1,0:T(8,128)(2,1)}, u32[]{:S(2)}) copy-start(bf16[2048,256]{1,0:T(8,128)(2,1)} %basis_h.1) | copy-start | bytes 3145732
  1.2 1.0 %copy-start.1 = (bf16[1,3,256,256]{3,2,1,0:T(8,128)(2,1)S(1)}, bf16[1,3,256,256]{3,2,1,0:T(8,128)(2,1)}, u32[]{:S(2)}) copy-start(bf16[1,3,256,256]{3,2,1,0:T(8,128)(2,1)} %coupling_h.1) | copy-start | bytes 1179652
  2.2 0.9 %copy-start.2 = (f32[32,2048]{1,0:T(8,128)S(1)}, f32[32,2048]{1,0:T(8,128)}, u32[]{:S(2)}) copy-start(f32[32,2048]{1,0:T(8,128)} %iterate_h.1) | copy-start | bytes 786436
  3.2 0.9 %copy-start.3 = (f32[32,2048]{1,0:T(8,128)S(1)}, f32[32,2048]{1,0:T(8,128)}, u32[]{:S(2)}) copy-start(f32[32,2048]{1,0:T(8,128)} %target_h.1) | copy-start | bytes 786436
  4.1 0.9 %copy-start.4 = (bf16[1,2,256,256]{3,2,1,0:T(8,128)(2,1)S(1)}, bf16[1,2,256,256]{3,2,1,0:T(8,128)(2,1)}, u32[]{:S(2)}) copy-start(bf16[1,2,256,256]{3,2,1,0:T(8,128)(2,1)} %transfer_h.1) | copy-start | bytes 786436
  5.1 0.8 %copy-start.5 = (s32[3,2048]{1,0:T(4,128)S(1)}, s32[3,2048]{1,0:T(4,128)}, u32[]{:S(2)}) copy-start(s32[3,2048]{1,0:T(4,128)} %coords_h.1) | copy-start | bytes 73732
  5.8 0.7 %copy-start.6 = (s32[1,2048]{1,0:T(1,128)S(1)}, s32[1,2048]{1,0:T(1,128)}, u32[]{:S(2)}) copy-start(s32[1,2048]{1,0:T(1,128)} %order_h.1) | copy-start | bytes 24580

commit v3 on v2

--- a/solution.py
+++ b/solution.py
@@ -290,7 +290,7 @@
             dma((n,)), dma((n,)), dma((n,)), dma((n,)), dma((n,)), dma((n,)),
         ],
         compiler_params=pltpu.CompilerParams(
-            collective_id=0, has_side_effects=True, vmem_limit_bytes=50 * 2**20
+            collective_id=0, has_side_effects=True, vmem_limit_bytes=60 * 2**20
         ),
     )(iterate, target, coords, tree_order, leaf_basis, transfer, coupling)
 

time: 45 us -> 39.9 us (0.89)
  local copies, waits for them, and re-layouts: 7.23 us -> 1.67 us
  Pallas kernels: 37.4 us -> 38 us
    unnamed x15 -> x1, local copies, waits for them, and re-layouts: 7.23 us -> 1.67 us
    pallas_call x1, Pallas kernels: 37.4 us -> 38 us  [fused_local(): pl.pallas_call(functools.partial(fused, n, levels), out_shape=jax.ShapeDt...]
where the time goes in v3:
time: 39.9 us; the launch traced here: 39.7 us
  Pallas kernels  38 us (95%)
  local copies, waits for them, and re-layouts  1.67 us (4%)
    pallas_call x1, Pallas kernels, fused_local(): pl.pallas_call(functools.partial(fused, n, levels), out_shape=jax.ShapeDt...  38 us
    unnamed x1, local copies, waits for them, and re-layouts  1.67 us

profile of v3, /device:TPU:0, one launch (start us, length us, event | category | flops | bytes accessed | tf_op | source)
XLA Modules:
  0.0 39.7 jit_solution(1198413499335275773)
XLA Ops:
  0.0 38.0 %shard_map.73 = f32[32,2048]{1,0:T(8,128)} custom-call(f32[32,2048]{1,0:T(8,128)} %iterate_h.1, f32[32,2048]{1,0:T(8,128)} %target_h.1, s32[3,2048]{1,0:T(4,128)} %coords_h.1, s32[1,2048]{1,0:T(1,128)} %order_h.1, bf16[2048,256]{1,0:T(8,128)(2,1)} %basis_h.1, bf16[1,2,256,256]{3,2,1,0:T(8,128)(2,1)} %transfer_h.1, bf16[1,3,256,256]{3,2,1,0:T(8,128)(2,1)} %coupling_h.1), custom_call_target="tpu_custom_call" | custom-call | tf_op jit(solution)/shard_map/pallas_call | solution.py:257
  38.0 1.7 %copy.9 = f32[32,2048]{1,0:T(8,128)} copy(f32[32,2048]{1,0:T(8,128)} %shard_map.73) | data formatting | bytes 524288

commit v4 on v3

--- a/solution.py
+++ b/solution.py
@@ -96,8 +96,10 @@
 
     for t in range(n):
         d = far_first(t, n)
-        spots = lax.broadcasted_iota(jnp.int32, (width, share), 0)
-        chosen = (spots == order[:, cols(peer(d))]).astype(F32).astype(BF16)
+        spots = lax.broadcasted_iota(jnp.int32, (width, share), 0).astype(jnp.int16)
+        wanted = jnp.broadcast_to(order[:, cols(peer(d))], (16, share)).astype(jnp.int16)
+        wanted = jnp.concatenate([wanted] * (width // 16), axis=0)
+        chosen = jnp.where(spots == wanted, jnp.ones((), BF16), jnp.zeros((), BF16))
         onehot[:, slot(d)] = chosen
         moved = jnp.dot(parts[...], chosen, preferred_element_type=F32)
         if d:
@@ -138,7 +140,7 @@
             s = q * lax.rsqrt(jnp.maximum(q, 1e-30))
             kernel_k[slot(i), slot(j)] = ((1.0 + s) * jnp.exp2(s * (-1.4426950408889634))).astype(BF16)
 
-    early = (5 * n) // 8
+    early = n
     for j in range(early):
         matern_column(j)
 

time: 39.9 us -> 39.7 us (level)
  no operation moved by 1% of the time
where the time goes in v4:
time: 39.7 us; the launch traced here: 39.5 us
  Pallas kernels  37.8 us (95%)
  local copies, waits for them, and re-layouts  1.67 us (4%)
    pallas_call x1, Pallas kernels, fused_local(): pl.pallas_call(functools.partial(fused, n, levels), out_shape=jax.ShapeDt...  37.8 us
    unnamed x1, local copies, waits for them, and re-layouts  1.67 us

profile of v4, /device:TPU:0, one launch (start us, length us, event | category | flops | bytes accessed | tf_op | source)
XLA Modules:
  0.0 39.5 jit_solution(15322119040570921727)
XLA Ops:
  0.0 37.8 %shard_map.73 = f32[32,2048]{1,0:T(8,128)} custom-call(f32[32,2048]{1,0:T(8,128)} %iterate_h.1, f32[32,2048]{1,0:T(8,128)} %target_h.1, s32[3,2048]{1,0:T(4,128)} %coords_h.1, s32[1,2048]{1,0:T(1,128)} %order_h.1, bf16[2048,256]{1,0:T(8,128)(2,1)} %basis_h.1, bf16[1,2,256,256]{3,2,1,0:T(8,128)(2,1)} %transfer_h.1, bf16[1,3,256,256]{3,2,1,0:T(8,128)(2,1)} %coupling_h.1), custom_call_target="tpu_custom_call" | custom-call | tf_op jit(solution)/shard_map/pallas_call | solution.py:259
  37.9 1.7 %copy.9 = f32[32,2048]{1,0:T(8,128)} copy(f32[32,2048]{1,0:T(8,128)} %shard_map.73) | data formatting | bytes 524288
